TPU v7x, 256 devices: a whole 4x4x8 slice. The times are simulated.
256 devices in a mesh: pipe: 16 (over y, x_lo, core), fsdp: 8 (over z), tp: 2 (over x_hi).
Axes of the slice: x: 4 (x_hi: 2, x_lo: 2; x = x_hi * 2 + x_lo), y: 4, z: 8, core: 2. Of those that a mesh axis runs over, the one named last changes fastest.
Arguments:
- act_in: bfloat16 [16, 2, 8, 128, 4096], P('pipe', None, 'fsdp', None, 'tp'), may hold values from -6 to 6
- gate_q: bfloat16 [16, 2, 8, 128, 4096], P('pipe', None, 'fsdp', None, 'tp'), may hold values from -6 to 6
- gate_k: bfloat16 [16, 2, 8, 128, 4096], P('pipe', None, 'fsdp', None, 'tp'), may hold values from -6 to 6
- grad_in: bfloat16 [16, 8, 128, 4096], P('pipe', 'fsdp', None, 'tp'), may hold values from -6 to 6
- weight: bfloat16 [16, 4096, 4096], P('pipe', 'tp', 'fsdp'), may hold values from -0.09375 to 0.09375
- filters: bfloat16 [16, 128, 256], P('pipe', None, 'tp'), may hold values from -0.5 to 0.5
Outputs:
- grad_out: bfloat16 [16, 2, 8, 128, 4096], P('pipe', None, 'fsdp', None, 'tp')
- filter_grad: float32 [16, 128, 256], P('pipe', 'fsdp', 'tp')
All inputs are finite; a program needn't handle non-finite values.
Results may differ from a plain program's by a relative error of at most 0.0056.
Values may be sent and summed in bfloat16 or wider, within the bound.
No kernel may reach another device: no remote copies, remote signals or barrier semaphores. Data moves between devices by JAX's collectives and lax.ppermute only.
A program may use at most 128 MiB of HBM per device.

v0:
```python
import math
import jax
import jax.numpy as jnp
from jax import lax
from jax.sharding import PartitionSpec as P


def passed_along(value, axis, by):
    peers = lax.axis_size(axis)
    pairs = [(i, i + by) for i in range(peers) if 0 <= i + by < peers]
    return lax.ppermute(value, axis, pairs)


def toeplitz(taps_table, seqlen):
    rows = taps_table.T
    padded = jnp.pad(rows, ((0, 0), (0, 2 * seqlen - rows.shape[1])))
    tiled = jnp.tile(padded, (1, seqlen))
    cut = tiled[:, : seqlen * (2 * seqlen - 1)].reshape(rows.shape[0], seqlen, 2 * seqlen - 1)
    return cut[:, :, :seqlen]


def filter_terms(adjoint, shaped, taps):
    seqlen = adjoint.shape[0]
    groups_loc = adjoint.shape[1]
    flipped = jnp.pad(shaped[::-1], ((0, taps), (0, 0), (0, 0)))
    span = seqlen + taps
    block = math.gcd(groups_loc, 16)
    pieces = []
    for first in range(0, groups_loc, block):
        corr = jnp.einsum(
            "tgc,ugc->gtu",
            adjoint[:, first : first + block],
            flipped[:, first : first + block],
            preferred_element_type=jnp.float32,
        )
        flat = corr.reshape(block, seqlen * span)[:, : seqlen * (span - 1)]
        skewed = flat.reshape(block, seqlen, span - 1)[:, :, seqlen - 1 : seqlen - 1 + taps]
        pieces.append(jnp.sum(skewed, axis=1))
    return jnp.concatenate(pieces, axis=0).T


def body(act_in, gate_q, gate_k, grad_in, weight, filters):
    ticks = act_in.shape[1]
    seqlen = act_in.shape[3]
    width_loc = act_in.shape[4]
    taps = filters.shape[1]
    groups_loc = filters.shape[2]
    per_group = width_loc // groups_loc
    scale = 1.0 / math.sqrt(ticks * lax.axis_size("fsdp") * seqlen * per_group)
    kernel = toeplitz(filters[0], seqlen)
    contract = (((1,), (1,)), ((), ()))
    incoming = grad_in[0, 0]
    outputs = []
    pending = jnp.zeros((taps, groups_loc), jnp.float32)
    for tick in range(ticks):
        if tick > 0:
            incoming = passed_along(outputs[-1], "pipe", -1)
        whole = lax.all_gather(incoming, "tp", axis=1, tiled=True)

        def add_panel(total, piece, start, whole=whole):
            return lax.dot_general(whole, piece, contract, preferred_element_type=jnp.float32)

        deriv = add_panel(
            jnp.zeros((seqlen, width_loc), jnp.float32),
            lax.all_gather(weight[0], "fsdp", axis=1, tiled=True),
            jnp.int32(0),
        )
        adjoint = (
            (gate_q[0, tick, 0] * deriv).astype(jnp.bfloat16).reshape(seqlen, groups_loc, per_group)
        )
        back = jnp.einsum(
            "gtu,ugc->tgc", kernel, adjoint, preferred_element_type=jnp.float32
        ).reshape(seqlen, width_loc)
        result = (incoming + gate_k[0, tick, 0] * back).astype(jnp.bfloat16)
        outputs.append(result)
        shaped = (
            gate_k[0, tick, 0].astype(jnp.float32) * act_in[0, tick, 0].astype(jnp.float32)
        ).astype(jnp.bfloat16)
        term = filter_terms(adjoint, shaped.reshape(seqlen, groups_loc, per_group), taps) * scale
        pending = pending + term
    summed = lax.psum_scatter(pending, "fsdp", scatter_dimension=0, tiled=True)
    grads = jnp.stack(outputs, axis=0)[None, :, None]
    return (grads, summed[None])


def solution(mesh):
    placed = (
        P("pipe", None, "fsdp", None, "tp"),
        P("pipe", None, "fsdp", None, "tp"),
        P("pipe", None, "fsdp", None, "tp"),
        P("pipe", "fsdp", None, "tp"),
        P("pipe", "tp", "fsdp"),
        P("pipe", None, "tp"),
    )
    return jax.shard_map(
        body,
        mesh=mesh,
        in_specs=placed,
        out_specs=(P("pipe", None, "fsdp", None, "tp"), P("pipe", "fsdp", "tp")),
        check_vma=False,
    )
```

profile of v0, /device:TPU:2, one launch (start us, length us, event | category | flops | bytes accessed | tf_op | source)
XLA Modules:
  0.0 514.4 jit_solution(2104143820232488051)
XLA Ops:
  8.9 3.8 tile.4
  12.7 12.3 %copy.61 = bf16[16,8,128,256]{3,1,2,0:T(8,128)(2,1)} copy(bf16[16,8,128,256]{3,2,1,0:T(8,128)(2,1)} %bitcast.136) | data formatting | bytes 16777216
  25.0 7.4 %slice.290 = bf16[128,32640]{1,0:T(8,128)(2,1)} slice(bf16[128,32768]{1,0:T(8,128)(2,1)} %bitcast.137), slice={[0:128], [0:32640]} | slice | bytes 16711680 | tf_op jit(solution)/shard_map/slice | solution.py:18
  32.4 29.8 %reshape.184 = bf16[128,128,255]{2,1,0:T(8,128)(2,1)} reshape(bf16[128,32640]{1,0:T(8,128)(2,1)} %slice.290) | data formatting | bytes 16711680 | tf_op jit(solution)/shard_map/reshape | solution.py:18
  64.0 150.7 %all-gather.10.cloned.1.call-done = bf16[1,2048,4096]{2,1,0:T(8,128)(2,1)} async-done(((bf16[1,2048,512]{2,1,0:T(8,128)(2,1)}), bf16[1,2048,4096]{2,1,0:T(8,128)(2,1)}) %all-gather.10.cloned.1.call-update) | async-done | bytes 16777232 | tf_op jit(solution)/shard_map/all_gather | solution.py:65
  214.7 11.8 %fusion.17 = bf16[128,2048]{1,0:T(8,128)(2,1)S(1)} fusion(bf16[1,2048,4096]{2,1,0:T(8,128)(2,1)} %all-gather.10.cloned.1.call-done, bf16[1,1,128,4096]{3,2,1,0:T(8,128)(2,1)} %all-gather.8.cloned.1.call-done, bf16[1,2,1,128,2048]{4,3,2,1,0:T(8,128)(2,1)S(1)} %copy-done.9), kind=kOutput, calls=%fused_computation.11 | convolution fusion | flops 2148270080 | bytes 18874368 | tf_op jit(solution)/shard_map/dot_general | solution.py:61
  247.9 6.2 %reshape.190 = f32[16,128,255]{2,1,0:T(8,128)} reshape(f32[16,32640]{1,0:T(8,128)} %slice.292) | data formatting | bytes 4177920 | tf_op jit(solution)/shard_map/reshape | solution.py:37
  260.4 6.1 %reshape.192 = f32[16,128,255]{2,1,0:T(8,128)} reshape(f32[16,32640]{1,0:T(8,128)} %slice.294) | data formatting | bytes 4177920 | tf_op jit(solution)/shard_map/reshape | solution.py:37
  272.7 6.1 %reshape.194 = f32[16,128,255]{2,1,0:T(8,128)} reshape(f32[16,32640]{1,0:T(8,128)} %slice.296) | data formatting | bytes 4177920 | tf_op jit(solution)/shard_map/reshape | solution.py:37
  285.5 6.1 %reshape.196 = f32[16,128,255]{2,1,0:T(8,128)} reshape(f32[16,32640]{1,0:T(8,128)} %slice.298) | data formatting | bytes 4177920 | tf_op jit(solution)/shard_map/reshape | solution.py:37
  297.8 6.3 %reshape.198 = f32[16,128,255]{2,1,0:T(8,128)} reshape(f32[16,32640]{1,0:T(8,128)} %slice.300) | data formatting | bytes 4177920 | tf_op jit(solution)/shard_map/reshape | solution.py:37
  310.3 6.1 %reshape.200 = f32[16,128,255]{2,1,0:T(8,128)} reshape(f32[16,32640]{1,0:T(8,128)} %slice.302) | data formatting | bytes 4177920 | tf_op jit(solution)/shard_map/reshape | solution.py:37
  326.3 6.2 %reshape.202 = f32[16,128,255]{2,1,0:T(8,128)} reshape(f32[16,32640]{1,0:T(8,128)} %slice.304) | data formatting | bytes 4177920 | tf_op jit(solution)/shard_map/reshape | solution.py:37
  336.9 6.1 %reshape.204 = f32[16,128,255]{2,1,0:T(8,128)} reshape(f32[16,32640]{1,0:T(8,128)} %slice.306) | data formatting | bytes 4177920 | tf_op jit(solution)/shard_map/reshape | solution.py:37
  349.5 12.0 %fusion.14 = bf16[128,2048]{1,0:T(8,128)(2,1)S(1)} fusion(bf16[128,4096]{1,0:T(8,128)(2,1)} %all-gather.6.cloned.1.call-done, bf16[1,2048,4096]{2,1,0:T(8,128)(2,1)} %all-gather.10.cloned.1.call-done, bf16[1,2,1,128,2048]{4,3,2,1,0:T(8,128)(2,1)} %param.7), kind=kOutput, calls=%fused_computation.10 | convolution fusion | flops 2148270080 | bytes 18874368 | tf_op jit(solution)/shard_map/dot_general | solution.py:61
  378.6 6.2 %reshape.206 = f32[16,128,255]{2,1,0:T(8,128)} reshape(f32[16,32640]{1,0:T(8,128)} %slice.308) | data formatting | bytes 4177920 | tf_op jit(solution)/shard_map/reshape | solution.py:37
  391.1 6.1 %reshape.208 = f32[16,128,255]{2,1,0:T(8,128)} reshape(f32[16,32640]{1,0:T(8,128)} %slice.310) | data formatting | bytes 4177920 | tf_op jit(solution)/shard_map/reshape | solution.py:37
  403.8 6.2 %reshape.210 = f32[16,128,255]{2,1,0:T(8,128)} reshape(f32[16,32640]{1,0:T(8,128)} %slice.312) | data formatting | bytes 4177920 | tf_op jit(solution)/shard_map/reshape | solution.py:37
  416.2 6.2 %reshape.212 = f32[16,128,255]{2,1,0:T(8,128)} reshape(f32[16,32640]{1,0:T(8,128)} %slice.314) | data formatting | bytes 4177920 | tf_op jit(solution)/shard_map/reshape | solution.py:37
  428.6 6.2 %reshape.214 = f32[16,128,255]{2,1,0:T(8,128)} reshape(f32[16,32640]{1,0:T(8,128)} %slice.316) | data formatting | bytes 4177920 | tf_op jit(solution)/shard_map/reshape | solution.py:37
  441.1 6.2 %reshape.216 = f32[16,128,255]{2,1,0:T(8,128)} reshape(f32[16,32640]{1,0:T(8,128)} %slice.318) | data formatting | bytes 4177920 | tf_op jit(solution)/shard_map/reshape | solution.py:37
  453.5 6.2 %reshape.218 = f32[16,128,255]{2,1,0:T(8,128)} reshape(f32[16,32640]{1,0:T(8,128)} %slice.320) | data formatting | bytes 4177920 | tf_op jit(solution)/shard_map/reshape | solution.py:37
  463.0 4.6 reshape.220
  473.2 32.9 %reduce-scatter.4.cloned.1.call-done = f32[16,128]{1,0:T(8,128)} async-done(((f32[128,128]{1,0:T(8,128)}), f32[16,128]{1,0:T(8,128)}) %reduce-scatter.4.cloned.1.call-update) | async-done | bytes 8208
  (145 shorter events, 141.9 us)
Async XLA Ops:
  7.2 1.5 copy-start.10
  7.2 56.8 %all-gather.8.cloned.1.call-start = ((), (), s32[]{:S(2)}) async-start(), calls=%async_computation.2 | async-start | bytes 1572864 | tf_op jit(solution)/shard_map/all_gather | solution.py:58
  7.9 206.8 %all-gather.10.cloned.1.call-start = ((), (), s32[]{:S(2)}) async-start(), calls=%async_computation.3 | async-start | bytes 18874368 | tf_op jit(solution)/shard_map/all_gather | solution.py:65
  8.7 340.8 %all-gather.6.cloned.1.call-start = ((), (), s32[]{:S(2)}) async-start(), calls=%async_computation.1 | async-start | bytes 1572864 | tf_op jit(solution)/shard_map/all_gather | solution.py:58
  32.4 29.8 %copy-start.1 = (bf16[1,2,1,128,2048]{4,3,2,1,0:T(8,128)(2,1)S(1)}, bf16[1,2,1,128,2048]{4,3,2,1,0:T(8,128)(2,1)}, u32[]{:S(2)}) copy-start(bf16[1,2,1,128,2048]{4,3,2,1,0:T(8,128)(2,1)} %param.8) | copy-start | bytes 3145732
  32.4 29.8 %copy-start.8 = (bf16[1,2,1,128,2048]{4,3,2,1,0:T(8,128)(2,1)S(1)}, bf16[1,2,1,128,2048]{4,3,2,1,0:T(8,128)(2,1)}, u32[]{:S(2)}) copy-start(bf16[1,2,1,128,2048]{4,3,2,1,0:T(8,128)(2,1)} %param.6) | copy-start | bytes 3145732
  62.6 152.1 %copy-start.9 = (bf16[1,2,1,128,2048]{4,3,2,1,0:T(8,128)(2,1)S(1)}, bf16[1,2,1,128,2048]{4,3,2,1,0:T(8,128)(2,1)}, u32[]{:S(2)}) copy-start(bf16[1,2,1,128,2048]{4,3,2,1,0:T(8,128)(2,1)} %param.7) | copy-start | bytes 3145732
  226.8 10.2 %slice-start = ((s8[8388608]{0:T(1024)(128)(4,1)}), s8[4194304]{0:T(1024)(128)(4,1)S(1)}, s32[]{:S(2)}) async-start(s8[8388608]{0:T(1024)(128)(4,1)} %bitcast.132), calls=%async_computation.5 | async-start | bytes 8388608
  231.8 5.1 slice-start.1
  239.2 1.3 copy-start.4
  240.5 4.7 copy-start
  243.1 78.7 %collective-permute-start = (bf16[128,2048]{1,0:T(8,128)(2,1)}, bf16[128,2048]{1,0:T(8,128)(2,1)}, u32[]{:S(2)}, u32[]{:S(2)}) collective-permute-start(bf16[128,2048]{1,0:T(8,128)(2,1)} %fusion.23), channel_id=1, source_target_pairs={{16,0},{32,16},{48,32},{64,48},{80,64},{96,80},{112,96},{128,112},... | collective-permute-start | bytes 1572872 | tf_op jit(solution)/shard_map/ppermute | solution.py:11
  321.8 184.3 %reduce-scatter.4.cloned.1.call-start = ((), (), s32[]{:S(2)}) async-start(), calls=%async_computation.4 | async-start | bytes 73728
  343.1 5.3 %copy-start.2 = (bf16[1,2,1,128,2048]{4,3,2,1,0:T(8,128)(2,1)S(1)}, bf16[1,2,1,128,2048]{4,3,2,1,0:T(8,128)(2,1)}, u32[]{:S(2)}) copy-start(bf16[1,2,1,128,2048]{4,3,2,1,0:T(8,128)(2,1)} %param.8) | copy-start | bytes 3145732
  344.4 4.0 copy-start.5
  363.7 8.8 %slice-start.2 = ((s8[8388608]{0:T(1024)(128)(4,1)}), s8[4194304]{0:T(1024)(128)(4,1)S(1)}, s32[]{:S(2)}) async-start(s8[8388608]{0:T(1024)(128)(4,1)} %bitcast.134), calls=%async_computation.7 | async-start | bytes 8388608
  368.8 3.8 slice-start.3
  463.0 7.5 %copy-start.6 = (f32[128,16,128]{2,1,0:T(8,128)S(1)}, f32[128,16,128]{2,1,0:T(8,128)}, u32[]{:S(2)}) copy-start(f32[128,16,128]{2,1,0:T(8,128)} %fusion.4) | copy-start | bytes 3145732
  467.6 3.2 copy-start.3
  470.8 1.3 copy-start.7
Sparse Core Ops, SparseCore 0:
  9.8 29.9 all-gather.7
  41.6 173.1 all-gather.9
  322.0 26.2 all-gather.5
  470.6 35.5 reduce-scatter.3
where the time goes:
time: 522 us; the launch traced here: 514 us
  local copies, waits for them, and re-layouts  221 us (42%)
  waiting for transfers between devices  185 us (35%)
  matrix products  53.6 us (10%)
  other arithmetic  37.5 us (7%)
  between operations  14.5 us (3%)
    all_gather x1, waiting for transfers between devices, body(): lax.all_gather(weight[0], 'fsdp', axis=1, tiled=True)  151 us
    reshape x16, local copies, waits for them, and re-layouts, filter_terms(): flat.reshape(block, seqlen, span - 1)[:, :, seqlen - 1:seqlen - 1 + taps]  97.1 us
    unnamed x65, local copies, waits for them, and re-layouts  56 us
    unnamed x5, waiting for transfers between devices  34.4 us
    reduce_sum x16, other arithmetic, filter_terms(): pieces.append(jnp.sum(skewed, axis=1))  31.1 us
    reshape x1, local copies, waits for them, and re-layouts, toeplitz(): tiled[:, :seqlen * (2 * seqlen - 1)]  29.8 us
    dot_general x16, matrix products, filter_terms(): jnp.einsum('tgc,ugc->gtu', adjoint[:, first:first + block], flipped[:, fi...  24.3 us
    dot_general x2, matrix products, add_panel(): lax.dot_general(whole, piece, contract, preferred_element_type=jnp.float32)  23.7 us
  transfers between devices with their start and end apart: 5, of which 2 were waited for; matrix products, arithmetic and copies ran while one was open for 31% of the time, Pallas kernels for 0%

commit v1 on v0

--- a/solution.py
+++ b/solution.py
@@ -3,6 +3,13 @@
 import jax.numpy as jnp
 from jax import lax
 from jax.sharding import PartitionSpec as P
+
+
+def swapped_in(x, name, along):
+    size = lax.axis_size(name)
+    tiles = jnp.stack([x for _ in range(size)])
+    tiles = lax.all_to_all(tiles, name, split_axis=0, concat_axis=0)
+    return jnp.concatenate(tiles, axis=along)
 
 
 def passed_along(value, axis, by):
@@ -62,7 +69,7 @@
 
         deriv = add_panel(
             jnp.zeros((seqlen, width_loc), jnp.float32),
-            lax.all_gather(weight[0], "fsdp", axis=1, tiled=True),
+            swapped_in(weight[0], "fsdp", 1),
             jnp.int32(0),
         )
         adjoint = (

time: 522 us -> 690 us (1.32)
  waiting for transfers between devices: 185 us -> 343 us
  local copies, waits for them, and re-layouts: 221 us -> 230 us
  starting transfers between devices: 2.45 us -> 11.1 us
    all_to_all x0 -> x1, waiting for transfers between devices: none -> 311 us  [swapped_in(): tiles = lax.all_to_all(tiles, name, split_axis=0, concat_axis=0)]
    all_gather x1 -> x0, waiting for transfers between devices: 151 us -> none  [body(): lax.all_gather(weight[0], 'fsdp', axis=1, tiled=True)]
    another operation x0 -> x2, local copies, waits for them, and re-layouts: none -> 8.91 us  [the longest x1 5.98 us: swapped_in(): tiles = jnp.stack([x for _ in range(size)])]
    all_to_all x0 -> x1, starting transfers between devices: none -> 8.6 us  [swapped_in(): tiles = lax.all_to_all(tiles, name, split_axis=0, concat_axis=0)]
    unnamed x5 -> x4, waiting for transfers between devices: 34.4 us -> 31.6 us
  transfers between devices with their start and end apart: 5 -> 5, of which waited for: 2 -> 2; matrix products, arithmetic and copies ran while one was open for 31% -> 24% of each run, Pallas kernels for 0% -> 0%
where the time goes in v1:
time: 690 us; the launch traced here: 682 us
  waiting for transfers between devices  343 us (50%)
  local copies, waits for them, and re-layouts  230 us (33%)
  matrix products  47 us (7%)
  other arithmetic  37.4 us (5%)
  between operations  14.5 us (2%)
  starting transfers between devices  11.1 us (2%)
    all_to_all x1, waiting for transfers between devices, swapped_in(): tiles = lax.all_to_all(tiles, name, split_axis=0, concat_axis=0)  311 us
    reshape x16, local copies, waits for them, and re-layouts, filter_terms(): flat.reshape(block, seqlen, span - 1)[:, :, seqlen - 1:seqlen - 1 + taps]  97.6 us
    unnamed x65, local copies, waits for them, and re-layouts  55.3 us
    unnamed x4, waiting for transfers between devices  31.6 us
    reduce_sum x16, other arithmetic, filter_terms(): pieces.append(jnp.sum(skewed, axis=1))  31.1 us
    reshape x1, local copies, waits for them, and re-layouts, toeplitz(): tiled[:, :seqlen * (2 * seqlen - 1)]  29.7 us
    dot_general x16, matrix products, filter_terms(): jnp.einsum('tgc,ugc->gtu', adjoint[:, first:first + block], flipped[:, fi...  24.5 us
    slice x16, local copies, waits for them, and re-layouts, filter_terms(): flat = corr.reshape(block, seqlen * span)[:, :seqlen * (span - 1)]  22.2 us
  transfers between devices with their start and end apart: 5, of which 2 were waited for; matrix products, arithmetic and copies ran while one was open for 24% of the time, Pallas kernels for 0%

profile of v1, /device:TPU:2, one launch (start us, length us, event | category | flops | bytes accessed | tf_op | source)
XLA Modules:
  0.0 682.4 jit_solution(12074562438394179487)
XLA Ops:
  10.1 6.0 stack.11
  16.1 8.6 %all-to-all-start = ((bf16[8,2048,512]{1,2,0:T(8,128)(2,1)}), bf16[8,2048,512]{1,2,0:T(8,128)(2,1)}, u32[]{:S(2)}, u32[]{:S(2)}) async-start(bf16[8,2048,512]{1,2,0:T(8,128)(2,1)} %stack.11), calls=%async_computation | async-start | bytes 33554432 | tf_op jit(solution)/shard_map/all_to_all | solution.py:11
  29.4 12.3 %copy.64 = bf16[16,8,128,256]{3,1,2,0:T(8,128)(2,1)} copy(bf16[16,8,128,256]{3,2,1,0:T(8,128)(2,1)} %bitcast.129) | data formatting | bytes 16777216
  41.7 7.3 %slice.290 = bf16[128,32640]{1,0:T(8,128)(2,1)} slice(bf16[128,32768]{1,0:T(8,128)(2,1)} %bitcast.130), slice={[0:128], [0:32640]} | slice | bytes 16711680 | tf_op jit(solution)/shard_map/slice | solution.py:25
  48.9 29.7 %reshape.195 = bf16[128,128,255]{2,1,0:T(8,128)(2,1)} reshape(bf16[128,32640]{1,0:T(8,128)(2,1)} %slice.290) | data formatting | bytes 16711680 | tf_op jit(solution)/shard_map/reshape | solution.py:25
  80.5 311.2 %all-to-all-done = bf16[8,2048,512]{1,2,0:T(8,128)(2,1)} async-done(((bf16[8,2048,512]{1,2,0:T(8,128)(2,1)}), bf16[8,2048,512]{1,2,0:T(8,128)(2,1)}, u32[]{:S(2)}, u32[]{:S(2)}) %all-to-all-start) | async-done | bytes 16777248 | tf_op jit(solution)/shard_map/all_to_all | solution.py:11
  391.7 8.4 %fusion.4 = bf16[128,2048]{1,0:T(8,128)(2,1)S(1)} fusion(bf16[2048,4096]{0,1:T(8,128)(2,1)} %bitcast.6, bf16[1,1,128,4096]{3,2,1,0:T(8,128)(2,1)} %all-gather.6.cloned.1.call-done, bf16[1,2,1,128,2048]{4,3,2,1,0:T(8,128)(2,1)S(1)} %copy-done.9), kind=kOutput, calls=%fused_computation.6 | convolution fusion | flops 2148270080 | bytes 18874368 | tf_op jit(solution)/shard_map/dot_general | solution.py:68
  421.7 6.1 reshape.201
  434.0 6.2 reshape.203
  446.5 6.2 reshape.205
  459.3 6.2 reshape.207
  471.7 6.1 reshape.209
  484.0 6.2 reshape.211
  500.0 6.1 reshape.213
  510.4 6.2 reshape.215
  523.0 8.4 %fusion.5 = bf16[128,2048]{1,0:T(8,128)(2,1)S(1)} fusion(bf16[128,4096]{1,0:T(8,128)(2,1)} %all-gather.4.cloned.1.call-done, bf16[2048,4096]{0,1:T(8,128)(2,1)} %bitcast.6, bf16[1,2,1,128,2048]{4,3,2,1,0:T(8,128)(2,1)} %param.7), kind=kOutput, calls=%fused_computation.7 | convolution fusion | flops 2148270080 | bytes 18874368 | tf_op jit(solution)/shard_map/dot_general | solution.py:68
  548.8 6.2 reshape.217
  561.2 6.1 reshape.219
  573.5 6.6 reshape.221
  586.4 6.2 reshape.223
  598.8 6.2 reshape.225
  611.2 6.3 reshape.227
  623.7 6.2 reshape.229
  643.4 30.9 %reduce-scatter.4.cloned.1.call-done = f32[16,128]{1,0:T(8,128)} async-done(((f32[128,128]{1,0:T(8,128)}), f32[16,128]{1,0:T(8,128)}) %reduce-scatter.4.cloned.1.call-update) | async-done | bytes 8208
  (146 shorter events, 152.1 us)
Async XLA Ops:
  16.1 9.4 %copy-start.10 = (bf16[1,128,128]{2,1,0:T(8,128)(2,1)S(1)}, bf16[1,128,128]{2,1,0:T(8,128)(2,1)}, u32[]{:S(2)}) copy-start(bf16[1,128,128]{2,1,0:T(8,128)(2,1)} %param.11) | copy-start | bytes 98308
  16.1 375.6 %all-to-all-start = ((bf16[8,2048,512]{1,2,0:T(8,128)(2,1)}), bf16[8,2048,512]{1,2,0:T(8,128)(2,1)}, u32[]{:S(2)}, u32[]{:S(2)}) async-start(bf16[8,2048,512]{1,2,0:T(8,128)(2,1)} %stack.11), calls=%async_computation | async-start | bytes 33554432 | tf_op jit(solution)/shard_map/all_to_all | solution.py:11
  24.7 55.8 %all-gather.6.cloned.1.call-start = ((), (), s32[]{:S(2)}) async-start(), calls=%async_computation.3 | async-start | bytes 1572864 | tf_op jit(solution)/shard_map/all_gather | solution.py:65
  25.4 497.5 %all-gather.4.cloned.1.call-start = ((), (), s32[]{:S(2)}) async-start(), calls=%async_computation.2 | async-start | bytes 1572864 | tf_op jit(solution)/shard_map/all_gather | solution.py:65
  48.9 29.7 %copy-start.1 = (bf16[1,2,1,128,2048]{4,3,2,1,0:T(8,128)(2,1)S(1)}, bf16[1,2,1,128,2048]{4,3,2,1,0:T(8,128)(2,1)}, u32[]{:S(2)}) copy-start(bf16[1,2,1,128,2048]{4,3,2,1,0:T(8,128)(2,1)} %param.8) | copy-start | bytes 3145732
  48.9 29.7 %copy-start.8 = (bf16[1,2,1,128,2048]{4,3,2,1,0:T(8,128)(2,1)S(1)}, bf16[1,2,1,128,2048]{4,3,2,1,0:T(8,128)(2,1)}, u32[]{:S(2)}) copy-start(bf16[1,2,1,128,2048]{4,3,2,1,0:T(8,128)(2,1)} %param.6) | copy-start | bytes 3145732
  79.1 312.6 %copy-start.9 = (bf16[1,2,1,128,2048]{4,3,2,1,0:T(8,128)(2,1)S(1)}, bf16[1,2,1,128,2048]{4,3,2,1,0:T(8,128)(2,1)}, u32[]{:S(2)}) copy-start(bf16[1,2,1,128,2048]{4,3,2,1,0:T(8,128)(2,1)} %param.7) | copy-start | bytes 3145732
  400.4 10.1 %slice-start = ((s8[8388608]{0:T(1024)(128)(4,1)}), s8[4194304]{0:T(1024)(128)(4,1)S(1)}, s32[]{:S(2)}) async-start(s8[8388608]{0:T(1024)(128)(4,1)} %bitcast.125), calls=%async_computation.5 | async-start | bytes 8388608
  405.5 5.0 slice-start.1
  412.8 1.3 copy-start.4
  414.2 4.8 copy-start
  416.7 78.8 %collective-permute-start = (bf16[128,2048]{1,0:T(8,128)(2,1)}, bf16[128,2048]{1,0:T(8,128)(2,1)}, u32[]{:S(2)}, u32[]{:S(2)}) collective-permute-start(bf16[128,2048]{1,0:T(8,128)(2,1)} %fusion.9), channel_id=1, source_target_pairs={{16,0},{32,16},{48,32},{64,48},{80,64},{96,80},{112,96},{128,112},... | collective-permute-start | bytes 1572872 | tf_op jit(solution)/shard_map/ppermute | solution.py:18
  495.5 178.7 %reduce-scatter.4.cloned.1.call-start = ((), (), s32[]{:S(2)}) async-start(), calls=%async_computation.4 | async-start | bytes 73728
  516.6 5.3 copy-start.2
  517.9 4.0 copy-start.5
  533.7 9.1 %slice-start.2 = ((s8[8388608]{0:T(1024)(128)(4,1)}), s8[4194304]{0:T(1024)(128)(4,1)S(1)}, s32[]{:S(2)}) async-start(s8[8388608]{0:T(1024)(128)(4,1)} %bitcast.127), calls=%async_computation.7 | async-start | bytes 8388608
  539.1 3.7 slice-start.3
  633.2 7.5 %copy-start.6 = (f32[128,16,128]{2,1,0:T(8,128)S(1)}, f32[128,16,128]{2,1,0:T(8,128)}, u32[]{:S(2)}) copy-start(f32[128,16,128]{2,1,0:T(8,128)} %fusion) | copy-start | bytes 3145732
  637.8 3.2 copy-start.3
  641.0 1.3 copy-start.7
Sparse Core Ops, SparseCore 0:
  27.3 28.6 all-gather.5
  495.7 23.9 all-gather.3
  640.8 33.4 reduce-scatter.3
